TPU v7x, 32 devices: a whole 2x2x4 slice. The times are simulated.
32 devices in a mesh: groups: 2 (over x), owner: 16 (over z, y, core).
Axes of the slice: x: 2, y: 2, z: 4, core: 2. Of those that a mesh axis runs over, the one named last changes fastest.
Arguments:
- features: bfloat16 [256, 384, 256], P(('groups', 'owner')), parts along dimension 0, may hold values from -8 to 8
- pairs: int32 [1280, 2], P(('groups', 'owner')), parts along dimension 0, may hold values from 0 to 127, as said below
Outputs:
- confidence: bfloat16 [256, 384], P(('groups', 'owner')), parts along dimension 0
There are 2 independent parts, one for each index of `groups`. A program takes and returns all parts, laid end to end along the dimension named above; each array names one. Nothing has to cross between parts.
Inputs may be any that keep to these rules, and one draw needn't show every extreme that they name: View v is held by owner index v // 8; pair row p is held by owner index p // 40. The 40 pairs of one device name exactly 40 distinct views, each in exactly two of its pairs and never twice in one pair. Among the views named by one device's pairs, the count held by any one owner is at most 3, and for one owner it equals 3 at every device.
All inputs are finite; a program needn't handle non-finite values.
Results may differ from a plain program's by a relative error of at most 0.001.
Values may be sent and summed in bfloat16 or wider, within the bound.
No kernel may reach another device: no remote copies, remote signals or barrier semaphores. Data moves between devices by JAX's collectives and lax.ppermute only.
A program may use at most 128 MiB of HBM per device.

v0:
```python
import functools
import math

import jax
import jax.numpy as jnp
import numpy as np
from jax import lax
from jax.experimental import pallas as pl
from jax.experimental.pallas import tpu as pltpu
from jax.sharding import PartitionSpec as P

LANES = 128
SUM_LOW, SUM_HIGH = 1e-28, 1e36


PIECES = 2
GROUP = 2


def small_slice_moves():
    at = lambda z, y, c: (z * 2 + y) * 2 + c
    yc = [(y, c) for y in range(2) for c in range(2)]
    step = lambda z, t: [(at(z, y, c), at(t, y, c)) for y, c in yc]
    return dict(
        near=step(1, 2) + step(0, 1),
        high=step(3, 2) + step(2, 3),
        side=[(at(z, y, c), at(z, 1 - y, c)) for z in range(4) for y, c in yc],
        far=step(0, 2),
        cross=[(at(3, 1 - y, c), at(2, y, c)) for y, c in yc],
        core=[(i, i ^ 1) for i in range(16)],
    )


SMALL_FLOWS = [
    (0, "near"),
    (0, "high"),
    (0, "side"),
    (0, "far"),
    (0, "cross"),
    (1, "core"),
    (2, "core"),
    (3, "core"),
    (4, "core"),
]
EARLY = [(0, 0), (0, 1), (3, 0), (3, 1), (8, 0), (8, 1), (2, 0), (2, 1), (7, 0), (7, 1), (1, 0), (1, 1), (6, 0), (6, 1)]
SMALL_PHASES = [
    EARLY + [(5, 0), (4, 0), (9, 0)],
    [(4, 1), (9, 1)] + EARLY + [(5, 0), (5, 1), (4, 0), (9, 0)],
]


def cyclic_distances(owners):
    step = max(1, math.isqrt(owners // 2))
    reach = set(range(step))
    top = step - 1
    while top < owners // 2:
        top += step
        reach.add(top)
    return sorted({d % owners for d in reach} - {0})


@functools.lru_cache(None)
def make_plan(owners):
    if owners == 16:
        moves = small_slice_moves()
        flows = [(source, moves[name]) for source, name in SMALL_FLOWS]
        phases = SMALL_PHASES
    else:
        flows = [(0, [((i + d) % owners, i) for i in range(owners)]) for d in cyclic_distances(owners)]
        phases = [[(k, piece) for k in range(len(flows) + 1) for piece in range(PIECES)]]
    held = [[d] for d in range(owners)]
    for source, perm in flows:
        arrived = {t: held[s][source] for s, t in perm}
        for d in range(owners):
            held[d].append(arrived.get(d, -1))
    first = [{} for _ in range(owners)]
    for d in range(owners):
        for k, o in enumerate(held[d]):
            if o >= 0:
                first[d].setdefault(o, k)
    table = np.zeros((owners, owners, owners), np.int32)
    load = np.zeros(owners)
    choices = []
    for a in range(owners):
        for b in range(a, owners):
            at = [d for d in range(owners) if a in first[d] and b in first[d]]
            assert at
            choices.append((len(at), a, b, at))
    for _, a, b, at in sorted(choices):
        d = min(at, key=lambda d: (load[d], d))
        load[d] += 1 if a == b else 2
        table[d, a, b] = first[d][a] * 64 + first[d][b] + 1
        table[d, b, a] = first[d][b] * 64 + first[d][a] + 1
    order = np.full((len(phases), (len(flows) + 1) * PIECES), -1, np.int32)
    for phase, pieces in enumerate(phases):
        for place, (k, piece) in enumerate(pieces):
            order[phase, k * PIECES + piece] = place
    return flows, phases, table, order


def pair_lists(pairs, mine, order, views_dev):
    count, owners = pairs.shape[0], mine.shape[0]
    left, right = pairs[:, 0], pairs[:, 1]
    is_left = (left // views_dev)[:, None] == jnp.arange(owners)[None, :]
    is_right = (right // views_dev)[:, None] == jnp.arange(owners)[None, :]
    row = jnp.dot(is_left.astype(jnp.float32), mine.astype(jnp.float32), precision=lax.Precision.HIGHEST)
    found = jnp.sum(jnp.where(is_right, row, 0.0), axis=1).astype(jnp.int32)
    buffers = jnp.maximum(found - 1, 0)
    deep = views_dev // PIECES
    left_piece = (buffers // 64) * PIECES + (left % views_dev) // deep
    right_piece = (buffers % 64) * PIECES + (right % views_dev) // deep
    place = jnp.arange(count)
    free = found > 0
    lists = []
    for phase in range(order.shape[0]):
        where = jnp.asarray(order[phase])[None, :]
        names = jnp.arange(order.shape[1])[None, :]
        left_at = jnp.sum(jnp.where(left_piece[:, None] == names, where, 0), axis=1)
        right_at = jnp.sum(jnp.where(right_piece[:, None] == names, where, 0), axis=1)
        chosen = free & (left_at >= 0) & (right_at >= 0)
        free = free & jnp.logical_not(chosen)
        key = jnp.maximum(left_at, right_at) * count + place
        rank = jnp.sum((key[None, :] < key[:, None]) & chosen[None, :], axis=1)
        picker = (rank[None, :] == place[:, None]) & chosen[None, :]
        slots = (left_at * deep + left % deep) * 1024 + right_at * deep + right % deep
        slots = jnp.sum(jnp.where(picker, slots[None, :], 0), axis=1)
        views = jnp.sum(jnp.where(picker, (left * 1024 + right)[None, :], 0), axis=1)
        lists.append((jnp.sum(chosen.astype(jnp.int32)).reshape(1), slots, views))
    return lists


def kernel(pieces, score_scale, count_ref, slots_ref, views_ref, before_ref, *refs):
    sources = refs[:-7]
    out_ref, arena, held, by_row, by_col, bounds, sems = refs[-7:]
    length = arena.shape[1]
    deep = arena.shape[0] // len(pieces)
    total = count_ref[0]
    limit = slots_ref.shape[0] - 1

    def slots_of(p):
        packed = slots_ref[jnp.minimum(p, limit)]
        return lax.shift_right_logical(packed, 10), lax.bitwise_and(packed, 1023)

    def wait_until(needed, waited):
        def wait(k, carry):
            part = arena.at[pl.ds(0, deep)]
            pltpu.make_async_copy(part, part, sems.at[k]).wait()
            return carry

        lax.fori_loop(waited, needed, wait, 0)
        return jnp.maximum(waited, needed)

    def product(p):
        left, right = slots_of(p)
        return lax.dot_general(
            arena[left], arena[right], (((1,), (1,)), ((), ())), preferred_element_type=jnp.float32
        )

    def record(p, row_conf, col_conf):
        packed = views_ref[jnp.minimum(p, limit)]
        real = p < total
        left = jnp.where(real, lax.shift_right_logical(packed, 10), -1)
        right = jnp.where(real, lax.bitwise_and(packed, 1023), by_row.shape[1])
        for tile in range(by_row.shape[1] // LANES):
            lane = lax.broadcasted_iota(jnp.int32, (length, LANES), 1) + tile * LANES
            at = (slice(None), slice(tile * LANES, (tile + 1) * LANES))
            by_row[at] = jnp.maximum(by_row[at], jnp.where(lane == left, row_conf, 0.0))
        by_col[pl.ds(right, 1), :] = jnp.maximum(by_col[pl.ds(right, 1), :], col_conf)

    def plain(p, scores):
        weight = jnp.exp2(scores[...] * (score_scale / math.log(2.0)))
        row_sum = jnp.sum(weight, axis=1, keepdims=True)
        col_sum = jnp.sum(weight, axis=0, keepdims=True)
        least = jnp.minimum(jnp.min(row_sum, axis=0, keepdims=True), jnp.min(col_sum, axis=1, keepdims=True))
        most = jnp.maximum(jnp.max(row_sum, axis=0, keepdims=True), jnp.max(col_sum, axis=1, keepdims=True))
        bounds[0] = jnp.minimum(bounds[0], jnp.where(p < total, least, 1.0))
        bounds[1] = jnp.maximum(bounds[1], jnp.where(p < total, most, 1.0))
        row_inv, col_inv = lax.rsqrt(row_sum), lax.rsqrt(col_sum)
        row_top = jnp.max(weight * col_inv, axis=1, keepdims=True) * row_inv
        col_top = jnp.max(weight * row_inv, axis=0, keepdims=True) * col_inv
        record(p, row_top * row_top, col_top * col_top)

    def shifted(p, carry):
        held[0] = product(p) * score_scale
        value = held[0]
        row_peak = jnp.max(value, axis=1, keepdims=True)
        row_total = row_peak + jnp.log(jnp.sum(jnp.exp(value - row_peak), axis=1, keepdims=True))
        col_peak = jnp.max(value, axis=0, keepdims=True)
        col_total = col_peak + jnp.log(jnp.sum(jnp.exp(value - col_peak), axis=0, keepdims=True))
        value = (value - row_total) + (value - col_total)
        record(p, jnp.exp(jnp.max(value, axis=1, keepdims=True)), jnp.exp(jnp.max(value, axis=0, keepdims=True)))
        return carry

    def clear():
        by_row[...] = jnp.zeros_like(by_row)
        by_col[...] = jnp.zeros_like(by_col)

    for place, (source, first) in enumerate(pieces):
        pltpu.make_async_copy(
            sources[source].at[pl.ds(first, deep)], arena.at[pl.ds(place * deep, deep)], sems.at[place]
        ).start()
    clear()
    bounds[...] = jnp.ones_like(bounds)

    def load(first, at, waited):
        needed = 1
        for g in range(GROUP):
            left, right = slots_of(first + g)
            needed = jnp.maximum(needed, lax.div(jnp.maximum(left, right), deep) + 1)
        waited = wait_until(needed, waited)
        for g in range(GROUP):
            held[at * GROUP + g] = product(first + g)
        return waited

    def rounds(k, waited):
        first = 2 * GROUP * k
        for at in range(2):
            waited = load(first + (at + 1) * GROUP, 1 - at, waited)
            for g in range(GROUP):
                plain(first + at * GROUP + g, held.at[at * GROUP + g])
        return waited

    waited = load(0, 0, jnp.int32(0))
    waited = lax.fori_loop(0, lax.div(total + 2 * GROUP - 1, 2 * GROUP), rounds, waited)
    wait_until(jnp.int32(len(pieces)), waited)
    fine = (jnp.min(bounds[0]) >= SUM_LOW) & (jnp.max(bounds[1]) <= SUM_HIGH)

    @pl.when(jnp.logical_not(fine))
    def again():
        clear()
        lax.fori_loop(0, total, shifted, 0)

    result = jnp.maximum(by_row[...].T, by_col[: by_row.shape[1], :]).astype(jnp.bfloat16)
    out_ref[...] = jnp.maximum(result, before_ref[...])


def confidences(lists, before, sources, pieces, deep, score_scale, work):
    count, slots, views = lists
    padded, length = before.shape
    width = sources[0].shape[2]
    smem = pl.BlockSpec(memory_space=pltpu.SMEM)
    vmem = pl.BlockSpec(memory_space=pltpu.VMEM)
    return pl.pallas_call(
        functools.partial(kernel, pieces, score_scale),
        out_shape=jax.ShapeDtypeStruct(before.shape, jnp.bfloat16),
        in_specs=[smem] * 3 + [vmem] + [pl.BlockSpec(memory_space=pl.ANY)] * len(sources),
        out_specs=vmem,
        scratch_shapes=[
            pltpu.VMEM((len(pieces) * deep, length, width), jnp.bfloat16),
            pltpu.VMEM((2 * GROUP, length, length), jnp.float32),
            pltpu.VMEM((length, padded), jnp.float32),
            pltpu.VMEM((padded + 8, length), jnp.float32),
            pltpu.VMEM((2, 1, 1), jnp.float32),
            pltpu.SemaphoreType.DMA((len(pieces),)),
        ],
        compiler_params=pltpu.CompilerParams(vmem_limit_bytes=56 * 1024 * 1024),
        cost_estimate=pl.CostEstimate(flops=work, bytes_accessed=0, transcendentals=0),
    )(count, slots, views, before, *sources)


def gather_small_slice(features, pairs, moves):
    send = lambda x, name: lax.ppermute(x, "owner", moves[name])
    tie = lax.optimization_barrier
    half = features.shape[0] // PIECES
    halves = [features[:half], features[half:]]
    flat = pairs.reshape(1, -1)
    shift = lambda s: [(i, (i + 4 * s) % 16) for i in range(16)]
    flat = jnp.concatenate([flat] + [lax.ppermute(flat, "owner", shift(s)) for s in (1, 2, 3)])
    halves, flat = tie((halves, flat))
    near, high = [send(x, "near") for x in halves], [send(x, "high") for x in halves]
    flat = jnp.concatenate([flat, send(flat, "side")])
    own, flat = tie((features, flat))
    side = send(own, "side")
    flat = jnp.concatenate([flat, send(flat, "core")])
    far, cross = [], []
    for k in range(PIECES):
        mine, near[k], high[k] = tie((halves[k], near[k], high[k]))
        far.append(send(mine, "far"))
        cross.append(send(mine, "cross"))
    swapped = lambda parts: [send(x, "core") for x in parts]
    buffers = [[features], near, high, [side], far, cross, swapped(near), swapped(high), swapped([side]), swapped(far[:1]) + far[1:]]
    return flat.reshape(-1, 2), buffers


def local(features, pairs):
    owners = lax.axis_size("owner")
    views_dev, length, width = features.shape
    flows, phases, table, order = make_plan(owners)
    if owners == 16:
        everyone, buffers = gather_small_slice(features, pairs, small_slice_moves())
    else:
        everyone = lax.all_gather(pairs, "owner", axis=0, tiled=True)
        buffers = [[features]] + [[lax.ppermute(features, "owner", perm)] for _, perm in flows]
    mine = jnp.asarray(table)[lax.axis_index("owner")]
    lists = pair_lists(everyone, mine, order, views_dev)
    deep = views_dev // PIECES
    padded = (owners * views_dev + LANES - 1) // LANES * LANES
    best = jnp.zeros((padded, length), jnp.bfloat16)
    for phase, (listed, wanted) in enumerate(zip(lists, phases)):
        sources, pieces = [], []
        if phase > 0:
            far, best = lax.optimization_barrier((buffers[4][1], best))
            buffers[9][1] = lax.ppermute(far, "owner", small_slice_moves()["core"])
        for k, piece in wanted:
            part = buffers[k][piece] if len(buffers[k]) > 1 else buffers[k][0]
            if not any(part is x for x in sources):
                sources.append(part)
            at = [part is x for x in sources].index(True)
            pieces.append((at, 0 if len(buffers[k]) > 1 else piece * deep))
        best = confidences(listed, best, sources, tuple(pieces), deep, 10.0 / width, 10**8)
    outgoing = best[: owners * views_dev].reshape(owners, views_dev, length)
    returned = lax.all_to_all(outgoing, "owner", split_axis=0, concat_axis=0, tiled=True)
    return jnp.max(returned, axis=0)


def solution(mesh):
    placed = (P(("groups", "owner"), None, None), P(("groups", "owner"), None))
    return jax.shard_map(
        local, mesh=mesh, in_specs=placed, out_specs=P(("groups", "owner"), None), check_vma=False
    )
```

profile of v0, /device:TPU:2, one launch (start us, length us, event | category | flops | bytes accessed | tf_op | source)
XLA Modules:
  0.0 198.9 jit_solution(2238838684647543273)
XLA Ops:
  0.0 0.8 copy.15
  0.9 3.7 %collective-permute-start.2 = (s32[1,80]{1,0:T(1,128)S(1)}, s32[1,80]{1,0:T(1,128)S(1)}, u32[]{:S(2)}, u32[]{:S(2)}) collective-permute-start(s32[1,80]{1,0:T(1,128)S(1)} %reshape.245), channel_id=1, source_target_pairs={{0,12},{1,13},{2,14},{3,15},{4,0},{5,1},{6,2},{7,3},{8,4},{9,5},{1... | collective-permute-start | bytes 968 | tf_op jit(solution)/shard_map/ppermute | solution.py:268
  4.5 1.0 collective-permute-start
  5.6 2.6 %fusion.30 = (bf16[4,384,256]{2,1,0:T(8,128)(2,1)}, bf16[4,384,256]{2,1,0:T(8,128)(2,1)}) fusion(bf16[8,384,256]{2,1,0:T(8,128)(2,1)} %refs_2_.1), kind=kLoop, calls=%fused_computation.99 | loop fusion | bytes 3145728 | tf_op jit(solution)/shard_map/slice | solution.py:265
  8.2 0.8 collective-permute-done.1
  9.0 0.9 collective-permute-done
  9.9 1.6 collective-permute-start.3
  11.5 2.1 %collective-permute-done.3 = s32[4,80]{1,0:T(4,128)S(1)} collective-permute-done((s32[4,80]{1,0:T(4,128)S(1)}, s32[4,80]{1,0:T(4,128)S(1)}, u32[]{:S(2)}, u32[]{:S(2)}) %collective-permute-start.3) | collective-permute-done | bytes 1312 | tf_op jit(solution)/shard_map/ppermute | solution.py:262
  13.6 1.6 collective-permute-start.8
  15.2 1.5 collective-permute-start.11
  16.7 3.6 %collective-permute-start.10 = (bf16[4,384,256]{2,1,0:T(8,128)(2,1)}, bf16[4,384,256]{2,1,0:T(8,128)(2,1)}, u32[]{:S(2)}, u32[]{:S(2)}) collective-permute-start(bf16[4,384,256]{2,1,0:T(8,128)(2,1)} %get-tuple-element.28), channel_id=1, source_target_pairs={{4,8},{5,9},{6,10},{7,11},{0,4},{1,5},{2,6},{3,7},{20,24},{21,25},... | collective-permute-start | bytes 2359304 | tf_op jit(solution)/shard_map/ppermute | solution.py:262
  20.3 1.5 collective-permute-start.6
  21.9 3.7 %collective-permute-start.5 = (bf16[4,384,256]{2,1,0:T(8,128)(2,1)}, bf16[4,384,256]{2,1,0:T(8,128)(2,1)}, u32[]{:S(2)}, u32[]{:S(2)}) collective-permute-start(bf16[4,384,256]{2,1,0:T(8,128)(2,1)} %get-tuple-element.21), channel_id=1, source_target_pairs={{4,8},{5,9},{6,10},{7,11},{0,4},{1,5},{2,6},{3,7},{20,24},{21,25},... | collective-permute-start | bytes 2359304 | tf_op jit(solution)/shard_map/ppermute | solution.py:262
  26.4 1.1 fusion.2
  27.5 10.0 %collective-permute-done.10.refs_7_.refs_9_ = bf16[4,384,256]{2,1,0:T(8,128)(2,1)} collective-permute-done((bf16[4,384,256]{2,1,0:T(8,128)(2,1)}, bf16[4,384,256]{2,1,0:T(8,128)(2,1)}, u32[]{:S(2)}, u32[]{:S(2)}) %collective-permute-start.10) | collective-permute-done | bytes 786464 | tf_op jit(solution)/shard_map/ppermute | solution.py:262
  37.5 5.7 %collective-permute-start.17 = (bf16[4,384,256]{2,1,0:T(8,128)(2,1)}, bf16[4,384,256]{2,1,0:T(8,128)(2,1)S(1)}, u32[]{:S(2)}, u32[]{:S(2)}) collective-permute-start(bf16[4,384,256]{2,1,0:T(8,128)(2,1)} %get-tuple-element.28), channel_id=1, source_target_pairs={{0,8},{1,9},{2,10},{3,11},{16,24},{17,25},{18,26},{19,27}} | collective-permute-start | bytes 2359304 | tf_op jit(solution)/shard_map/ppermute | solution.py:262
  43.3 0.7 collective-permute-start.16
  44.0 10.4 %collective-permute-done.5.refs_8_.refs_10_ = bf16[4,384,256]{2,1,0:T(8,128)(2,1)} collective-permute-done((bf16[4,384,256]{2,1,0:T(8,128)(2,1)}, bf16[4,384,256]{2,1,0:T(8,128)(2,1)}, u32[]{:S(2)}, u32[]{:S(2)}) %collective-permute-start.5) | collective-permute-done | bytes 786464 | tf_op jit(solution)/shard_map/ppermute | solution.py:262
  55.0 1.1 slice_reduce_fusion.1
  56.9 6.4 %collective-permute-start.7 = (bf16[4,384,256]{2,1,0:T(8,128)(2,1)}, bf16[4,384,256]{2,1,0:T(8,128)(2,1)}, u32[]{:S(2)}, u32[]{:S(2)}) collective-permute-start(bf16[4,384,256]{2,1,0:T(8,128)(2,1)} %get-tuple-element.21), channel_id=1, source_target_pairs={{0,8},{1,9},{2,10},{3,11},{16,24},{17,25},{18,26},{19,27}} | collective-permute-start | bytes 2359304 | tf_op jit(solution)/shard_map/ppermute | solution.py:262
  63.3 8.0 %collective-permute-done.17.refs_12_.refs_15_ = bf16[4,384,256]{2,1,0:T(8,128)(2,1)S(1)} collective-permute-done((bf16[4,384,256]{2,1,0:T(8,128)(2,1)}, bf16[4,384,256]{2,1,0:T(8,128)(2,1)S(1)}, u32[]{:S(2)}, u32[]{:S(2)}) %collective-permute-start.17) | collective-permute-done | bytes 786464 | tf_op jit(solution)/shard_map/ppermute | solution.py:262
  71.8 0.7 iota_add_fusion.1
  73.8 2.1 %select_reduce_fusion = (s32[640]{0:T(1024)}, s32[640]{0:T(1024)}, s32[640]{0:T(1024)}, s32[640]{0:T(1024)}) fusion(s32[640]{0:T(1024)S(1)} %get-tuple-element.70, s32[640]{0:T(1024)S(1)} %get-tuple-element.67, pred[640]{0:T(1024)(128)(4,1)S(1)} %get-tuple-element.65, s32[640]{0:T(1024)S(1)} %get-tuple-element.62, s32[640]{0:T(1024)S(1)} %get-tuple-element.61, ...), kind=kLoop, calls=%fused_computation | loop fusion | flops 4912640 | bytes 24320 | tf_op jit(solution)/shard_map/reduce_sum | solution.py:127
  75.9 1.5 collective-permute-start.20
  77.4 0.9 copy-done.9
  78.4 0.7 broadcast_in_dim.97.before_ref
  79.6 13.6 %shard_map.55.before_ref = bf16[128,384]{1,0:T(8,128)(2,1)} custom-call(s32[1]{0:T(128)} %bitcast.2.count_ref, s32[640]{0:T(1024)} %get-tuple-element.40.slots_ref, s32[640]{0:T(1024)} %get-tuple-element.39.views_ref, bf16[128,384]{1,0:T(8,128)(2,1)} %broadcast_in_dim.97.before_ref, bf16[8,384,256]{2,1,0:T(8,128)(2,1)} %refs_2_.1, ...), custom_call_target="tpu_custom_call" | custom-call | flops 100000000 | tf_op jit(solution)/shard_map/pallas_call | solution.py:243
  93.2 1.7 collective-permute-start.19
  94.9 2.1 %collective-permute-done.19.refs_1_ = bf16[4,384,256]{2,1,0:T(8,128)(2,1)S(1)} collective-permute-done((bf16[4,384,256]{2,1,0:T(8,128)(2,1)}, bf16[4,384,256]{2,1,0:T(8,128)(2,1)S(1)}, u32[]{:S(2)}, u32[]{:S(2)}) %collective-permute-start.19) | collective-permute-done | bytes 786464 | tf_op jit(solution)/shard_map/ppermute | solution.py:303
  97.0 0.9 copy-done.10
  97.9 8.0 %shard_map.56 = bf16[128,384]{1,0:T(8,128)(2,1)} custom-call(s32[1]{0:T(128)} %bitcast.1.count_ref, s32[640]{0:T(1024)} %get-tuple-element.43.slots_ref, s32[640]{0:T(1024)} %get-tuple-element.44.views_ref, bf16[128,384]{1,0:T(8,128)(2,1)} %shard_map.55.before_ref, bf16[4,384,256]{2,1,0:T(8,128)(2,1)} %collective-permute-done.7.refs_0_, ...), custom_call_target="tpu_custom_call" | custom-call | flops 100000000 | tf_op jit(solution)/shard_map/pallas_call | solution.py:243
  105.9 92.3 %all_to_all.5 = bf16[16,8,384]{2,1,0:T(8,128)(2,1)S(1)} all-to-all(bf16[16,8,384]{2,1,0:T(8,128)(2,1)} %bitcast.6), channel_id=1, replica_groups=mesh['groups'=2,'owner'=16] {'owner'}, dimensions={0} | all-to-all | bytes 196608 | tf_op jit(solution)/shard_map/all_to_all | solution.py:312
  (58 shorter events, 5.2 us)
Async XLA Ops:
  0.9 12.7 %copy-start = (bf16[8,384,256]{2,1,0:T(8,128)(2,1)S(1)}, bf16[8,384,256]{2,1,0:T(8,128)(2,1)}, u32[]{:S(2)}) copy-start(bf16[8,384,256]{2,1,0:T(8,128)(2,1)} %refs_2_.1) | copy-start | bytes 4718596
  0.9 7.3 %collective-permute-start.2 = (s32[1,80]{1,0:T(1,128)S(1)}, s32[1,80]{1,0:T(1,128)S(1)}, u32[]{:S(2)}, u32[]{:S(2)}) collective-permute-start(s32[1,80]{1,0:T(1,128)S(1)} %reshape.245), channel_id=1, source_target_pairs={{0,12},{1,13},{2,14},{3,15},{4,0},{5,1},{6,2},{7,3},{8,4},{9,5},{1... | collective-permute-start | bytes 968 | tf_op jit(solution)/shard_map/ppermute | solution.py:268
  4.5 4.4 %collective-permute-start.1 = (s32[1,80]{1,0:T(1,128)S(1)}, s32[1,80]{1,0:T(1,128)S(1)}, u32[]{:S(2)}, u32[]{:S(2)}) collective-permute-start(s32[1,80]{1,0:T(1,128)S(1)} %reshape.245), channel_id=1, source_target_pairs={{0,8},{1,9},{2,10},{3,11},{4,12},{5,13},{6,14},{7,15},{8,0},{9,1},... | collective-permute-start | bytes 968 | tf_op jit(solution)/shard_map/ppermute | solution.py:268
  4.5 5.3 %collective-permute-start = (s32[1,80]{1,0:T(1,128)S(1)}, s32[1,80]{1,0:T(1,128)S(1)}, u32[]{:S(2)}, u32[]{:S(2)}) collective-permute-start(s32[1,80]{1,0:T(1,128)S(1)} %reshape.245), channel_id=1, source_target_pairs={{0,4},{1,5},{2,6},{3,7},{4,8},{5,9},{6,10},{7,11},{8,12},{9,13},{1... | collective-permute-start | bytes 968 | tf_op jit(solution)/shard_map/ppermute | solution.py:268
  8.2 47.9 %copy-start.11 = (s32[20]{0:T(128)S(1)}, s32[20]{0:T(128)}, u32[]{:S(2)}) copy-start(s32[20]{0:T(128)} %constant.130.clone) | copy-start | bytes 244
  8.2 47.9 %copy-start.12 = (s32[20]{0:T(128)S(1)}, s32[20]{0:T(128)}, u32[]{:S(2)}) copy-start(s32[20]{0:T(128)} %constant.129.clone) | copy-start | bytes 244
  9.9 3.7 %collective-permute-start.3 = (s32[4,80]{1,0:T(4,128)S(1)}, s32[4,80]{1,0:T(4,128)S(1)}, u32[]{:S(2)}, u32[]{:S(2)}) collective-permute-start(s32[4,80]{1,0:T(4,128)S(1)} %pad_add_fusion.2), channel_id=1, source_target_pairs={{0,2},{1,3},{2,0},{3,1},{4,6},{5,7},{6,4},{7,5},{8,10},{9,11},{10,... | collective-permute-start | bytes 3848 | tf_op jit(solution)/shard_map/ppermute | solution.py:262
  13.6 41.3 %collective-permute-start.8 = (bf16[8,384,256]{2,1,0:T(8,128)(2,1)S(1)}, bf16[8,384,256]{2,1,0:T(8,128)(2,1)S(1)}, u32[]{:S(2)}, u32[]{:S(2)}) collective-permute-start(bf16[8,384,256]{2,1,0:T(8,128)(2,1)S(1)} %copy-done), channel_id=1, source_target_pairs={{0,2},{1,3},{2,0},{3,1},{4,6},{5,7},{6,4},{7,5},{8,10},{9,11},{10,... | collective-permute-start | bytes 4718600 | tf_op jit(solution)/shard_map/ppermute | solution.py:262
  15.2 6.7 %collective-permute-start.4 = (s32[8,80]{1,0:T(8,128)S(1)}, s32[8,80]{1,0:T(8,128)S(1)}, u32[]{:S(2)}, u32[]{:S(2)}) collective-permute-start(s32[8,80]{1,0:T(8,128)S(1)} %pad_add_fusion.1), channel_id=1, source_target_pairs={{0,1},{1,0},{2,3},{3,2},{4,5},{5,4},{6,7},{7,6},{8,9},{9,8},{10,11... | collective-permute-start | bytes 7688 | tf_op jit(solution)/shard_map/ppermute | solution.py:262
  15.2 12.4 %collective-permute-start.11 = (bf16[4,384,256]{2,1,0:T(8,128)(2,1)}, bf16[4,384,256]{2,1,0:T(8,128)(2,1)}, u32[]{:S(2)}, u32[]{:S(2)}) collective-permute-start(bf16[4,384,256]{2,1,0:T(8,128)(2,1)} %get-tuple-element.28), channel_id=1, source_target_pairs={{12,8},{13,9},{14,10},{15,11},{8,12},{9,13},{10,14},{11,15},{28,24... | collective-permute-start | bytes 2359304 | tf_op jit(solution)/shard_map/ppermute | solution.py:262
  16.7 20.8 %collective-permute-start.10 = (bf16[4,384,256]{2,1,0:T(8,128)(2,1)}, bf16[4,384,256]{2,1,0:T(8,128)(2,1)}, u32[]{:S(2)}, u32[]{:S(2)}) collective-permute-start(bf16[4,384,256]{2,1,0:T(8,128)(2,1)} %get-tuple-element.28), channel_id=1, source_target_pairs={{4,8},{5,9},{6,10},{7,11},{0,4},{1,5},{2,6},{3,7},{20,24},{21,25},... | collective-permute-start | bytes 2359304 | tf_op jit(solution)/shard_map/ppermute | solution.py:262
  20.3 23.7 %collective-permute-start.6 = (bf16[4,384,256]{2,1,0:T(8,128)(2,1)}, bf16[4,384,256]{2,1,0:T(8,128)(2,1)}, u32[]{:S(2)}, u32[]{:S(2)}) collective-permute-start(bf16[4,384,256]{2,1,0:T(8,128)(2,1)} %get-tuple-element.21), channel_id=1, source_target_pairs={{12,8},{13,9},{14,10},{15,11},{8,12},{9,13},{10,14},{11,15},{28,24... | collective-permute-start | bytes 2359304 | tf_op jit(solution)/shard_map/ppermute | solution.py:262
  21.9 32.5 %collective-permute-start.5 = (bf16[4,384,256]{2,1,0:T(8,128)(2,1)}, bf16[4,384,256]{2,1,0:T(8,128)(2,1)}, u32[]{:S(2)}, u32[]{:S(2)}) collective-permute-start(bf16[4,384,256]{2,1,0:T(8,128)(2,1)} %get-tuple-element.21), channel_id=1, source_target_pairs={{4,8},{5,9},{6,10},{7,11},{0,4},{1,5},{2,6},{3,7},{20,24},{21,25},... | collective-permute-start | bytes 2359304 | tf_op jit(solution)/shard_map/ppermute | solution.py:262
  37.5 33.8 %collective-permute-start.17 = (bf16[4,384,256]{2,1,0:T(8,128)(2,1)}, bf16[4,384,256]{2,1,0:T(8,128)(2,1)S(1)}, u32[]{:S(2)}, u32[]{:S(2)}) collective-permute-start(bf16[4,384,256]{2,1,0:T(8,128)(2,1)} %get-tuple-element.28), channel_id=1, source_target_pairs={{0,8},{1,9},{2,10},{3,11},{16,24},{17,25},{18,26},{19,27}} | collective-permute-start | bytes 2359304 | tf_op jit(solution)/shard_map/ppermute | solution.py:262
  43.3 28.0 %collective-permute-start.16 = (bf16[4,384,256]{2,1,0:T(8,128)(2,1)}, bf16[4,384,256]{2,1,0:T(8,128)(2,1)S(1)}, u32[]{:S(2)}, u32[]{:S(2)}) collective-permute-start(bf16[4,384,256]{2,1,0:T(8,128)(2,1)} %get-tuple-element.28), channel_id=1, source_target_pairs={{14,8},{15,9},{12,10},{13,11},{30,24},{31,25},{28,26},{29,27}} | collective-permute-start | bytes 2359304 | tf_op jit(solution)/shard_map/ppermute | solution.py:262
  54.4 2.5 %collective-permute-start.13 = (bf16[4,384,256]{2,1,0:T(8,128)(2,1)}, bf16[4,384,256]{2,1,0:T(8,128)(2,1)S(1)}, u32[]{:S(2)}, u32[]{:S(2)}) collective-permute-start(bf16[4,384,256]{2,1,0:T(8,128)(2,1)} %collective-permute-done.6.refs_4_.refs_6_), channel_id=1, source_target_pairs={{0,1},{1,0},{2,3},{3,2},{4,5},{5,4},{6,7},{7,6},{8,9},{9,8},{10,11... | collective-permute-start | bytes 2359304 | tf_op jit(solution)/shard_map/ppermute | solution.py:262
  54.4 8.9 %collective-permute-start.15 = (bf16[4,384,256]{2,1,0:T(8,128)(2,1)}, bf16[4,384,256]{2,1,0:T(8,128)(2,1)S(1)}, u32[]{:S(2)}, u32[]{:S(2)}) collective-permute-start(bf16[4,384,256]{2,1,0:T(8,128)(2,1)} %collective-permute-done.5.refs_8_.refs_10_), channel_id=1, source_target_pairs={{0,1},{1,0},{2,3},{3,2},{4,5},{5,4},{6,7},{7,6},{8,9},{9,8},{10,11... | collective-permute-start | bytes 2359304 | tf_op jit(solution)/shard_map/ppermute | solution.py:262
  54.9 24.2 %copy-start.1 = (bf16[8,384,256]{2,1,0:T(8,128)(2,1)}, bf16[8,384,256]{2,1,0:T(8,128)(2,1)S(1)}, u32[]{:S(2)}) copy-start(bf16[8,384,256]{2,1,0:T(8,128)(2,1)S(1)} %collective-permute-done.8.refs_1_.refs_3_) | copy-start | bytes 4718596
  54.9 22.5 %collective-permute-start.9 = (bf16[8,384,256]{2,1,0:T(8,128)(2,1)S(1)}, bf16[8,384,256]{2,1,0:T(8,128)(2,1)S(1)}, u32[]{:S(2)}, u32[]{:S(2)}) collective-permute-start(bf16[8,384,256]{2,1,0:T(8,128)(2,1)S(1)} %collective-permute-done.8.refs_1_.refs_3_), channel_id=1, source_target_pairs={{0,1},{1,0},{2,3},{3,2},{4,5},{5,4},{6,7},{7,6},{8,9},{9,8},{10,11... | collective-permute-start | bytes 4718600 | tf_op jit(solution)/shard_map/ppermute | solution.py:262
  56.9 22.2 %copy-start.5 = (bf16[4,384,256]{2,1,0:T(8,128)(2,1)}, bf16[4,384,256]{2,1,0:T(8,128)(2,1)S(1)}, u32[]{:S(2)}) copy-start(bf16[4,384,256]{2,1,0:T(8,128)(2,1)S(1)} %collective-permute-done.13.refs_6_.refs_8_) | copy-start | bytes 2359300
  56.9 36.3 %collective-permute-start.7 = (bf16[4,384,256]{2,1,0:T(8,128)(2,1)}, bf16[4,384,256]{2,1,0:T(8,128)(2,1)}, u32[]{:S(2)}, u32[]{:S(2)}) collective-permute-start(bf16[4,384,256]{2,1,0:T(8,128)(2,1)} %get-tuple-element.21), channel_id=1, source_target_pairs={{0,8},{1,9},{2,10},{3,11},{16,24},{17,25},{18,26},{19,27}} | collective-permute-start | bytes 2359304 | tf_op jit(solution)/shard_map/ppermute | solution.py:262
  63.3 15.8 %copy-start.6 = (bf16[4,384,256]{2,1,0:T(8,128)(2,1)}, bf16[4,384,256]{2,1,0:T(8,128)(2,1)S(1)}, u32[]{:S(2)}) copy-start(bf16[4,384,256]{2,1,0:T(8,128)(2,1)S(1)} %collective-permute-done.15.refs_10_.refs_12_) | copy-start | bytes 2359300
  63.3 12.6 %collective-permute-start.12 = (bf16[4,384,256]{2,1,0:T(8,128)(2,1)}, bf16[4,384,256]{2,1,0:T(8,128)(2,1)S(1)}, u32[]{:S(2)}, u32[]{:S(2)}) collective-permute-start(bf16[4,384,256]{2,1,0:T(8,128)(2,1)} %collective-permute-done.11.refs_3_.refs_5_), channel_id=1, source_target_pairs={{0,1},{1,0},{2,3},{3,2},{4,5},{5,4},{6,7},{7,6},{8,9},{9,8},{10,11... | collective-permute-start | bytes 2359304 | tf_op jit(solution)/shard_map/ppermute | solution.py:262
  71.3 7.8 %copy-start.3 = (bf16[4,384,256]{2,1,0:T(8,128)(2,1)}, bf16[4,384,256]{2,1,0:T(8,128)(2,1)S(1)}, u32[]{:S(2)}) copy-start(bf16[4,384,256]{2,1,0:T(8,128)(2,1)S(1)} %collective-permute-done.17.refs_12_.refs_15_) | copy-start | bytes 2359300
  71.3 6.1 %collective-permute-start.14 = (bf16[4,384,256]{2,1,0:T(8,128)(2,1)}, bf16[4,384,256]{2,1,0:T(8,128)(2,1)S(1)}, u32[]{:S(2)}, u32[]{:S(2)}) collective-permute-start(bf16[4,384,256]{2,1,0:T(8,128)(2,1)} %collective-permute-done.10.refs_7_.refs_9_), channel_id=1, source_target_pairs={{0,1},{1,0},{2,3},{3,2},{4,5},{5,4},{6,7},{7,6},{8,9},{9,8},{10,11... | collective-permute-start | bytes 2359304 | tf_op jit(solution)/shard_map/ppermute | solution.py:262
  71.3 7.8 %copy-start.4 = (bf16[4,384,256]{2,1,0:T(8,128)(2,1)}, bf16[4,384,256]{2,1,0:T(8,128)(2,1)S(1)}, u32[]{:S(2)}) copy-start(bf16[4,384,256]{2,1,0:T(8,128)(2,1)S(1)} %collective-permute-done.16.refs_11_.refs_13_) | copy-start | bytes 2359300
  71.3 6.1 %collective-permute-start.18 = (bf16[4,384,256]{2,1,0:T(8,128)(2,1)S(1)}, bf16[4,384,256]{2,1,0:T(8,128)(2,1)S(1)}, u32[]{:S(2)}, u32[]{:S(2)}) collective-permute-start(bf16[4,384,256]{2,1,0:T(8,128)(2,1)S(1)} %collective-permute-done.17.refs_12_.refs_15_), channel_id=1, source_target_pairs={{0,1},{1,0},{2,3},{3,2},{4,5},{5,4},{6,7},{7,6},{8,9},{9,8},{10,11... | collective-permute-start | bytes 2359304 | tf_op jit(solution)/shard_map/ppermute | solution.py:262
  75.9 3.2 %copy-start.7 = (bf16[4,384,256]{2,1,0:T(8,128)(2,1)}, bf16[4,384,256]{2,1,0:T(8,128)(2,1)S(1)}, u32[]{:S(2)}) copy-start(bf16[4,384,256]{2,1,0:T(8,128)(2,1)S(1)} %collective-permute-done.12.refs_5_.refs_7_) | copy-start | bytes 2359300
  75.9 19.0 %collective-permute-start.20 = (bf16[4,384,256]{2,1,0:T(8,128)(2,1)}, bf16[4,384,256]{2,1,0:T(8,128)(2,1)}, u32[]{:S(2)}, u32[]{:S(2)}) collective-permute-start(bf16[4,384,256]{2,1,0:T(8,128)(2,1)} %get-tuple-element.21), channel_id=1, source_target_pairs={{14,8},{15,9},{12,10},{13,11},{30,24},{31,25},{28,26},{29,27}} | collective-permute-start | bytes 2359304 | tf_op jit(solution)/shard_map/ppermute | solution.py:262
  77.4 1.7 copy-start.8
  78.4 1.2 copy-start.2
  93.2 3.9 %collective-permute-start.19 = (bf16[4,384,256]{2,1,0:T(8,128)(2,1)}, bf16[4,384,256]{2,1,0:T(8,128)(2,1)S(1)}, u32[]{:S(2)}, u32[]{:S(2)}) collective-permute-start(bf16[4,384,256]{2,1,0:T(8,128)(2,1)} %collective-permute-done.7.refs_0_), channel_id=1, source_target_pairs={{0,1},{1,0},{2,3},{3,2},{4,5},{5,4},{6,7},{7,6},{8,9},{9,8},{10,11... | collective-permute-start | bytes 2359304 | tf_op jit(solution)/shard_map/ppermute | solution.py:303
  (2 other events, 1.9 us)
where the time goes:
time: 202 us; the launch traced here: 199 us
  blocking collectives  92.3 us (46%)
  starting transfers between devices  35.4 us (18%)
  waiting for transfers between devices  35 us (17%)
  Pallas kernels  21.5 us (11%)
  local copies, waits for them, and re-layouts  6.67 us (3%)
  other arithmetic  6.61 us (3%)
    all_to_all x1, blocking collectives, local(): lax.all_to_all(outgoing, 'owner', split_axis=0, concat_axis=0, tiled=True)  92.3 us
    ppermute x17, waiting for transfers between devices, gather_small_slice(): send = lambda x, name: lax.ppermute(x, 'owner', moves[name])  31.2 us
    ppermute x17, starting transfers between devices, gather_small_slice(): send = lambda x, name: lax.ppermute(x, 'owner', moves[name])  29 us
    pallas_call x2, Pallas kernels, confidences(): pl.pallas_call(functools.partial(kernel, pieces, score_scale), out_shape=...  21.5 us
    ppermute x3, starting transfers between devices, gather_small_slice(): lax.ppermute(flat, 'owner', shift(s))  4.67 us
  transfers between devices with their start and end apart: 21, of which 8 were waited for; matrix products, arithmetic and copies ran while one was open for 5% of the time, Pallas kernels for 7%

commit v1 on v0

--- a/solution.py
+++ b/solution.py
@@ -44,7 +44,8 @@
 ]
 EARLY = [(0, 0), (0, 1), (3, 0), (3, 1), (8, 0), (8, 1), (2, 0), (2, 1), (7, 0), (7, 1), (1, 0), (1, 1), (6, 0), (6, 1)]
 SMALL_PHASES = [
-    EARLY + [(5, 0), (4, 0), (9, 0)],
+    EARLY,
+    [(4, 0), (9, 0)] + EARLY + [(5, 0)],
     [(4, 1), (9, 1)] + EARLY + [(5, 0), (5, 1), (4, 0), (9, 0)],
 ]
 
@@ -125,7 +126,9 @@
         slots = (left_at * deep + left % deep) * 1024 + right_at * deep + right % deep
         slots = jnp.sum(jnp.where(picker, slots[None, :], 0), axis=1)
         views = jnp.sum(jnp.where(picker, (left * 1024 + right)[None, :], 0), axis=1)
-        lists.append((jnp.sum(chosen.astype(jnp.int32)).reshape(1), slots, views))
+        used = ((left_at[:, None] == names) | (right_at[:, None] == names)) & chosen[:, None]
+        counts = jnp.concatenate([jnp.sum(chosen.astype(jnp.int32)).reshape(1), jnp.any(used, axis=0).astype(jnp.int32)])
+        lists.append((counts, slots, views))
     return lists
 
 
@@ -144,7 +147,7 @@
     def wait_until(needed, waited):
         def wait(k, carry):
             part = arena.at[pl.ds(0, deep)]
-            pltpu.make_async_copy(part, part, sems.at[k]).wait()
+            pl.when(count_ref[k + 1] > 0)(lambda: pltpu.make_async_copy(part, part, sems.at[k]).wait())
             return carry
 
         lax.fori_loop(waited, needed, wait, 0)
@@ -196,9 +199,10 @@
         by_col[...] = jnp.zeros_like(by_col)
 
     for place, (source, first) in enumerate(pieces):
-        pltpu.make_async_copy(
+        piece = pltpu.make_async_copy(
             sources[source].at[pl.ds(first, deep)], arena.at[pl.ds(place * deep, deep)], sems.at[place]
-        ).start()
+        )
+        pl.when(count_ref[place + 1] > 0)(piece.start)
     clear()
     bounds[...] = jnp.ones_like(bounds)
 
@@ -220,9 +224,12 @@
                 plain(first + at * GROUP + g, held.at[at * GROUP + g])
         return waited
 
-    waited = load(0, 0, jnp.int32(0))
-    waited = lax.fori_loop(0, lax.div(total + 2 * GROUP - 1, 2 * GROUP), rounds, waited)
-    wait_until(jnp.int32(len(pieces)), waited)
+    @pl.when(total > 0)
+    def all_pairs():
+        waited = load(0, 0, jnp.int32(0))
+        waited = lax.fori_loop(0, lax.div(total + 2 * GROUP - 1, 2 * GROUP), rounds, waited)
+        wait_until(jnp.int32(len(pieces)), waited)
+
     fine = (jnp.min(bounds[0]) >= SUM_LOW) & (jnp.max(bounds[1]) <= SUM_HIGH)
 
     @pl.when(jnp.logical_not(fine))
@@ -263,22 +270,25 @@
     tie = lax.optimization_barrier
     half = features.shape[0] // PIECES
     halves = [features[:half], features[half:]]
+    near, high = [send(halves[0], "near")], [send(halves[0], "high")]
     flat = pairs.reshape(1, -1)
-    shift = lambda s: [(i, (i + 4 * s) % 16) for i in range(16)]
-    flat = jnp.concatenate([flat] + [lax.ppermute(flat, "owner", shift(s)) for s in (1, 2, 3)])
-    halves, flat = tie((halves, flat))
-    near, high = [send(x, "near") for x in halves], [send(x, "high") for x in halves]
     flat = jnp.concatenate([flat, send(flat, "side")])
     own, flat = tie((features, flat))
     side = send(own, "side")
     flat = jnp.concatenate([flat, send(flat, "core")])
+    mine, flat = tie((halves[1], flat))
+    shift = lambda s: [(i, (i + 4 * s) % 16) for i in range(16)]
+    flat = jnp.concatenate([flat] + [lax.ppermute(flat, "owner", shift(s)) for s in (1, 2, 3)])
+    flat, near[0], high[0] = tie((flat, near[0], high[0]))
+    near.append(send(mine, "near"))
+    high.append(send(mine, "high"))
     far, cross = [], []
     for k in range(PIECES):
         mine, near[k], high[k] = tie((halves[k], near[k], high[k]))
         far.append(send(mine, "far"))
         cross.append(send(mine, "cross"))
     swapped = lambda parts: [send(x, "core") for x in parts]
-    buffers = [[features], near, high, [side], far, cross, swapped(near), swapped(high), swapped([side]), swapped(far[:1]) + far[1:]]
+    buffers = [[features], near, high, [side], far, cross, swapped(near), swapped(high), swapped([side]), list(far)]
     return flat.reshape(-1, 2), buffers
 
 
@@ -299,8 +309,8 @@
     for phase, (listed, wanted) in enumerate(zip(lists, phases)):
         sources, pieces = [], []
         if phase > 0:
-            far, best = lax.optimization_barrier((buffers[4][1], best))
-            buffers[9][1] = lax.ppermute(far, "owner", small_slice_moves()["core"])
+            far, best = lax.optimization_barrier((buffers[4][phase - 1], best))
+            buffers[9][phase - 1] = lax.ppermute(far, "owner", small_slice_moves()["core"])
         for k, piece in wanted:
             part = buffers[k][piece] if len(buffers[k]) > 1 else buffers[k][0]
             if not any(part is x for x in sources):

time: 202 us -> 214 us (1.059); the launches traced: 199 us -> 215 us
  starting transfers between devices: 35.4 us -> 78.5 us
  blocking collectives: 92.3 us -> 63.9 us
  other arithmetic: 6.61 us -> 12.6 us
  Pallas kernels: 21.5 us -> 18.9 us
    ppermute x17 -> x16, starting transfers between devices: 29 us -> 74.3 us  [gather_small_slice(): send = lambda x, name: lax.ppermute(x, 'owner', moves[name])]
    all_to_all x1, blocking collectives: 92.3 us -> 63.9 us  [local(): lax.all_to_all(outgoing, 'owner', split_axis=0, concat_axis=0, tiled=True)]
    ppermute x17 -> x16, waiting for transfers between devices: 31.2 us -> 22.3 us  [gather_small_slice(): send = lambda x, name: lax.ppermute(x, 'owner', moves[name])]
    ppermute x3, waiting for transfers between devices: 1.71 us -> 9.86 us  [gather_small_slice(): lax.ppermute(flat, 'owner', shift(s))]
    concatenate x0 -> x3, other arithmetic: none -> 3.74 us  [pair_lists(): jnp.concatenate([jnp.sum(chosen.astype(jnp.int32)).reshape(1), jnp.any(us...]
    pallas_call x2 -> x3, Pallas kernels: 21.5 us -> 18.9 us  [confidences(): pl.pallas_call(functools.partial(kernel, pieces, score_scale), out_shape=...]
  transfers between devices with their start and end apart: 21 -> 21, of which waited for: 8 -> 8; matrix products, arithmetic and copies ran while one was open for 5% -> 7% of each run, Pallas kernels for 7% -> 8%
where the time goes in v1:
time: 214 us; the launch traced here: 215 us
  starting transfers between devices  78.5 us (37%)
  blocking collectives  63.9 us (30%)
  waiting for transfers between devices  33.2 us (16%)
  Pallas kernels  18.9 us (9%)
  other arithmetic  12.6 us (6%)
  local copies, waits for them, and re-layouts  6.88 us (3%)
    ppermute x16, starting transfers between devices, gather_small_slice(): send = lambda x, name: lax.ppermute(x, 'owner', moves[name])  74.3 us
    all_to_all x1, blocking collectives, local(): lax.all_to_all(outgoing, 'owner', split_axis=0, concat_axis=0, tiled=True)  63.9 us
    ppermute x16, waiting for transfers between devices, gather_small_slice(): send = lambda x, name: lax.ppermute(x, 'owner', moves[name])  22.3 us
    pallas_call x3, Pallas kernels, confidences(): pl.pallas_call(functools.partial(kernel, pieces, score_scale), out_shape=...  18.9 us
    ppermute x3, waiting for transfers between devices, gather_small_slice(): lax.ppermute(flat, 'owner', shift(s))  9.86 us
  transfers between devices with their start and end apart: 21, of which 8 were waited for; matrix products, arithmetic and copies ran while one was open for 7% of the time, Pallas kernels for 8%

profile of v1, /device:TPU:2, one launch (start us, length us, event | category | flops | bytes accessed | tf_op | source)
XLA Modules:
  0.0 215.4 jit_solution(7598652345688062671)
XLA Ops:
  0.0 2.8 %fusion.40 = (bf16[4,384,256]{2,1,0:T(8,128)(2,1)}, bf16[4,384,256]{2,1,0:T(8,128)(2,1)}) fusion(bf16[8,384,256]{2,1,0:T(8,128)(2,1)} %refs_2_.3), kind=kLoop, calls=%fused_computation.129 | loop fusion | bytes 3145728 | tf_op jit(solution)/shard_map/slice | solution.py:272
  2.8 1.7 collective-permute-start.6
  4.4 4.4 %collective-permute-start.5 = (bf16[4,384,256]{2,1,0:T(8,128)(2,1)}, bf16[4,384,256]{2,1,0:T(8,128)(2,1)}, u32[]{:S(2)}, u32[]{:S(2)}) collective-permute-start(bf16[4,384,256]{2,1,0:T(8,128)(2,1)} %get-tuple-element.29), channel_id=1, source_target_pairs={{4,8},{5,9},{6,10},{7,11},{0,4},{1,5},{2,6},{3,7},{20,24},{21,25},... | collective-permute-start | bytes 2359304 | tf_op jit(solution)/shard_map/ppermute | solution.py:269
  9.0 1.6 collective-permute-start
  10.6 2.0 collective-permute-done
  12.6 1.6 collective-permute-start.11
  14.2 1.1 collective-permute-done.1
  15.4 1.7 collective-permute-start.4
  17.0 2.5 %collective-permute-start.3 = (s32[4,80]{1,0:T(4,128)S(1)}, s32[4,80]{1,0:T(4,128)S(1)}, u32[]{:S(2)}, u32[]{:S(2)}) collective-permute-start(s32[4,80]{1,0:T(4,128)S(1)} %pad_add_fusion.1), channel_id=1, source_target_pairs={{0,8},{1,9},{2,10},{3,11},{4,12},{5,13},{6,14},{7,15},{8,0},{9,1},... | collective-permute-start | bytes 3848 | tf_op jit(solution)/shard_map/ppermute | solution.py:281
  19.5 5.5 %collective-permute-done.4 = s32[4,80]{1,0:T(4,128)S(1)} collective-permute-done((s32[4,80]{1,0:T(4,128)S(1)}, s32[4,80]{1,0:T(4,128)S(1)}, u32[]{:S(2)}, u32[]{:S(2)}) %collective-permute-start.4) | collective-permute-done | bytes 1312 | tf_op jit(solution)/shard_map/ppermute | solution.py:281
  25.1 1.5 collective-permute-start.8
  26.6 4.3 %collective-permute-done.2 = s32[4,80]{1,0:T(4,128)S(1)} collective-permute-done((s32[4,80]{1,0:T(4,128)S(1)}, s32[4,80]{1,0:T(4,128)S(1)}, u32[]{:S(2)}, u32[]{:S(2)}) %collective-permute-start.2) | collective-permute-done | bytes 1312 | tf_op jit(solution)/shard_map/ppermute | solution.py:281
  30.9 2.2 %collective-permute-start.7 = (bf16[4,384,256]{2,1,0:T(8,128)(2,1)}, bf16[4,384,256]{2,1,0:T(8,128)(2,1)}, u32[]{:S(2)}, u32[]{:S(2)}) collective-permute-start(bf16[4,384,256]{2,1,0:T(8,128)(2,1)} %get-tuple-element.26), channel_id=1, source_target_pairs={{4,8},{5,9},{6,10},{7,11},{0,4},{1,5},{2,6},{3,7},{20,24},{21,25},... | collective-permute-start | bytes 2359304 | tf_op jit(solution)/shard_map/ppermute | solution.py:269
  33.3 4.6 %collective-permute-start.10 = (bf16[4,384,256]{2,1,0:T(8,128)(2,1)}, bf16[4,384,256]{2,1,0:T(8,128)(2,1)}, u32[]{:S(2)}, u32[]{:S(2)}) collective-permute-start(bf16[4,384,256]{2,1,0:T(8,128)(2,1)} %get-tuple-element.29), channel_id=1, source_target_pairs={{0,8},{1,9},{2,10},{3,11},{16,24},{17,25},{18,26},{19,27}} | collective-permute-start | bytes 2359304 | tf_op jit(solution)/shard_map/ppermute | solution.py:269
  38.6 1.1 fusion.3
  39.7 1.1 slice_reduce_fusion.1
  40.8 6.6 %collective-permute-done.11.refs_1_.refs_3_ = bf16[8,384,256]{2,1,0:T(8,128)(2,1)S(1)} collective-permute-done((bf16[8,384,256]{2,1,0:T(8,128)(2,1)S(1)}, bf16[8,384,256]{2,1,0:T(8,128)(2,1)S(1)}, u32[]{:S(2)}, u32[]{:S(2)}) %collective-permute-start.11) | collective-permute-done | bytes 1572896 | tf_op jit(solution)/shard_map/ppermute | solution.py:269
  47.6 0.9 convert_reduce_fusion.3
  51.2 1.3 pad_add_fusion.5.count_ref
  53.5 2.8 %select_reduce_fusion = (s32[640]{0:T(1024)}, s32[640]{0:T(1024)}, s32[640]{0:T(1024)}, s32[640]{0:T(1024)}, s32[640]{0:T(1024)}, /*index=5*/s32[640]{0:T(1024)}) fusion(s32[640]{0:T(1024)S(1)} %get-tuple-element.90, s32[640]{0:T(1024)S(1)} %get-tuple-element.85, pred[640]{0:T(1024)(128)(4,1)S(1)} %get-tuple-element.67, s32[640]{0:T(1024)S(1)} %get-tuple-element.83, ...), kind=kLoop, calls=%fused_computation | loop fusion | flops 7368960 | bytes 35200 | tf_op jit(solution)/shard_map/reduce_sum | solution.py:128
  57.0 0.7 broadcast_in_dim.140.before_ref
  58.7 15.0 %shard_map.64.before_ref = bf16[128,384]{1,0:T(8,128)(2,1)} custom-call(s32[21]{0:T(128)} %pad_add_fusion.5.count_ref, s32[640]{0:T(1024)} %get-tuple-element.48.slots_ref, s32[640]{0:T(1024)} %get-tuple-element.47.views_ref, bf16[128,384]{1,0:T(8,128)(2,1)} %broadcast_in_dim.140.before_ref, bf16[8,384,256]{2,1,0:T(8,128)(2,1)} %refs_2_.3, ...), custom_call_target="tpu_custom_call" | custom-call | flops 100000000 | tf_op jit(solution)/shard_map/pallas_call | solution.py:250
  73.8 54.5 %collective-permute-start.9 = (bf16[4,384,256]{2,1,0:T(8,128)(2,1)S(1)}, bf16[4,384,256]{2,1,0:T(8,128)(2,1)S(1)}, u32[]{:S(2)}, u32[]{:S(2)}) collective-permute-start(bf16[4,384,256]{2,1,0:T(8,128)(2,1)S(1)} %copy-done.12), channel_id=1, source_target_pairs={{0,8},{1,9},{2,10},{3,11},{16,24},{17,25},{18,26},{19,27}} | collective-permute-start | bytes 2359304 | tf_op jit(solution)/shard_map/ppermute | solution.py:269
  128.5 1.2 pad_add_fusion.4.count_ref
  130.5 0.9 copy-done.7
  131.6 2.0 shard_map.65.before_ref
  133.6 12.1 %collective-permute-done.9.refs_0_ = bf16[4,384,256]{2,1,0:T(8,128)(2,1)S(1)} collective-permute-done((bf16[4,384,256]{2,1,0:T(8,128)(2,1)S(1)}, bf16[4,384,256]{2,1,0:T(8,128)(2,1)S(1)}, u32[]{:S(2)}, u32[]{:S(2)}) %collective-permute-start.9) | collective-permute-done | bytes 786464 | tf_op jit(solution)/shard_map/ppermute | solution.py:269
  145.7 1.2 pad_add_fusion.3.count_ref
  147.0 1.1 collective-permute-done.19.refs_1_
  148.0 0.9 copy-done.11
  148.9 1.9 shard_map.66
  150.8 63.9 %all_to_all.5 = bf16[16,8,384]{2,1,0:T(8,128)(2,1)S(1)} all-to-all(bf16[16,8,384]{2,1,0:T(8,128)(2,1)} %bitcast.7), channel_id=1, replica_groups=mesh['groups'=2,'owner'=16] {'owner'}, dimensions={0} | all-to-all | bytes 196608 | tf_op jit(solution)/shard_map/all_to_all | solution.py:322
  (77 shorter events, 8.5 us)
Async XLA Ops:
  0.0 12.6 %copy-start = (bf16[8,384,256]{2,1,0:T(8,128)(2,1)S(1)}, bf16[8,384,256]{2,1,0:T(8,128)(2,1)}, u32[]{:S(2)}) copy-start(bf16[8,384,256]{2,1,0:T(8,128)(2,1)} %refs_2_.3) | copy-start | bytes 4718596
  0.0 8.8 %copy-start.13 = (s32[40,2]{0,1:T(2,128)S(1)}, s32[40,2]{0,1:T(2,128)}, u32[]{:S(2)}) copy-start(s32[40,2]{0,1:T(2,128)} %param.7) | copy-start | bytes 964
  2.8 44.7 %copy-start.14 = (s32[20]{0:T(128)S(1)}, s32[20]{0:T(128)}, u32[]{:S(2)}) copy-start(s32[20]{0:T(128)} %constant.141.clone) | copy-start | bytes 244
  2.8 44.7 %copy-start.15 = (s32[20]{0:T(128)S(1)}, s32[20]{0:T(128)}, u32[]{:S(2)}) copy-start(s32[20]{0:T(128)} %constant.140.clone) | copy-start | bytes 244
  2.8 44.7 %copy-start.16 = (s32[20]{0:T(128)S(1)}, s32[20]{0:T(128)}, u32[]{:S(2)}) copy-start(s32[20]{0:T(128)} %constant.139.clone) | copy-start | bytes 244
  2.8 30.4 %collective-permute-start.6 = (bf16[4,384,256]{2,1,0:T(8,128)(2,1)}, bf16[4,384,256]{2,1,0:T(8,128)(2,1)}, u32[]{:S(2)}, u32[]{:S(2)}) collective-permute-start(bf16[4,384,256]{2,1,0:T(8,128)(2,1)} %get-tuple-element.29), channel_id=1, source_target_pairs={{12,8},{13,9},{14,10},{15,11},{8,12},{9,13},{10,14},{11,15},{28,24... | collective-permute-start | bytes 2359304 | tf_op jit(solution)/shard_map/ppermute | solution.py:269
  4.4 28.7 %collective-permute-start.5 = (bf16[4,384,256]{2,1,0:T(8,128)(2,1)}, bf16[4,384,256]{2,1,0:T(8,128)(2,1)}, u32[]{:S(2)}, u32[]{:S(2)}) collective-permute-start(bf16[4,384,256]{2,1,0:T(8,128)(2,1)} %get-tuple-element.29), channel_id=1, source_target_pairs={{4,8},{5,9},{6,10},{7,11},{0,4},{1,5},{2,6},{3,7},{20,24},{21,25},... | collective-permute-start | bytes 2359304 | tf_op jit(solution)/shard_map/ppermute | solution.py:269
  9.0 3.6 %collective-permute-start = (s32[1,80]{1,0:T(1,128)S(1)}, s32[1,80]{1,0:T(1,128)S(1)}, u32[]{:S(2)}, u32[]{:S(2)}) collective-permute-start(s32[1,80]{1,0:T(1,128)S(1)} %reshape.367), channel_id=1, source_target_pairs={{0,2},{1,3},{2,0},{3,1},{4,6},{5,7},{6,4},{7,5},{8,10},{9,11},{10,... | collective-permute-start | bytes 968 | tf_op jit(solution)/shard_map/ppermute | solution.py:269
  12.6 34.8 %collective-permute-start.11 = (bf16[8,384,256]{2,1,0:T(8,128)(2,1)S(1)}, bf16[8,384,256]{2,1,0:T(8,128)(2,1)S(1)}, u32[]{:S(2)}, u32[]{:S(2)}) collective-permute-start(bf16[8,384,256]{2,1,0:T(8,128)(2,1)S(1)} %copy-done), channel_id=1, source_target_pairs={{0,2},{1,3},{2,0},{3,1},{4,6},{5,7},{6,4},{7,5},{8,10},{9,11},{10,... | collective-permute-start | bytes 4718600 | tf_op jit(solution)/shard_map/ppermute | solution.py:269
  14.2 1.1 collective-permute-start.1
  15.4 9.7 %collective-permute-start.4 = (s32[4,80]{1,0:T(4,128)S(1)}, s32[4,80]{1,0:T(4,128)S(1)}, u32[]{:S(2)}, u32[]{:S(2)}) collective-permute-start(s32[4,80]{1,0:T(4,128)S(1)} %pad_add_fusion.1), channel_id=1, source_target_pairs={{0,12},{1,13},{2,14},{3,15},{4,0},{5,1},{6,2},{7,3},{8,4},{9,5},{1... | collective-permute-start | bytes 3848 | tf_op jit(solution)/shard_map/ppermute | solution.py:281
  17.0 8.1 %collective-permute-start.3 = (s32[4,80]{1,0:T(4,128)S(1)}, s32[4,80]{1,0:T(4,128)S(1)}, u32[]{:S(2)}, u32[]{:S(2)}) collective-permute-start(s32[4,80]{1,0:T(4,128)S(1)} %pad_add_fusion.1), channel_id=1, source_target_pairs={{0,8},{1,9},{2,10},{3,11},{4,12},{5,13},{6,14},{7,15},{8,0},{9,1},... | collective-permute-start | bytes 3848 | tf_op jit(solution)/shard_map/ppermute | solution.py:281
  25.1 5.9 %collective-permute-start.2 = (s32[4,80]{1,0:T(4,128)S(1)}, s32[4,80]{1,0:T(4,128)S(1)}, u32[]{:S(2)}, u32[]{:S(2)}) collective-permute-start(s32[4,80]{1,0:T(4,128)S(1)} %pad_add_fusion.1), channel_id=1, source_target_pairs={{0,4},{1,5},{2,6},{3,7},{4,8},{5,9},{6,10},{7,11},{8,12},{9,13},{1... | collective-permute-start | bytes 3848 | tf_op jit(solution)/shard_map/ppermute | solution.py:281
  25.1 24.8 %collective-permute-start.8 = (bf16[4,384,256]{2,1,0:T(8,128)(2,1)}, bf16[4,384,256]{2,1,0:T(8,128)(2,1)}, u32[]{:S(2)}, u32[]{:S(2)}) collective-permute-start(bf16[4,384,256]{2,1,0:T(8,128)(2,1)} %get-tuple-element.26), channel_id=1, source_target_pairs={{12,8},{13,9},{14,10},{15,11},{8,12},{9,13},{10,14},{11,15},{28,24... | collective-permute-start | bytes 2359304 | tf_op jit(solution)/shard_map/ppermute | solution.py:269
  30.9 19.6 %collective-permute-start.7 = (bf16[4,384,256]{2,1,0:T(8,128)(2,1)}, bf16[4,384,256]{2,1,0:T(8,128)(2,1)}, u32[]{:S(2)}, u32[]{:S(2)}) collective-permute-start(bf16[4,384,256]{2,1,0:T(8,128)(2,1)} %get-tuple-element.26), channel_id=1, source_target_pairs={{4,8},{5,9},{6,10},{7,11},{0,4},{1,5},{2,6},{3,7},{20,24},{21,25},... | collective-permute-start | bytes 2359304 | tf_op jit(solution)/shard_map/ppermute | solution.py:269
  33.3 40.4 %collective-permute-start.10 = (bf16[4,384,256]{2,1,0:T(8,128)(2,1)}, bf16[4,384,256]{2,1,0:T(8,128)(2,1)}, u32[]{:S(2)}, u32[]{:S(2)}) collective-permute-start(bf16[4,384,256]{2,1,0:T(8,128)(2,1)} %get-tuple-element.29), channel_id=1, source_target_pairs={{0,8},{1,9},{2,10},{3,11},{16,24},{17,25},{18,26},{19,27}} | collective-permute-start | bytes 2359304 | tf_op jit(solution)/shard_map/ppermute | solution.py:269
  37.9 12.6 %collective-permute-start.13 = (bf16[4,384,256]{2,1,0:T(8,128)(2,1)}, bf16[4,384,256]{2,1,0:T(8,128)(2,1)S(1)}, u32[]{:S(2)}, u32[]{:S(2)}) collective-permute-start(bf16[4,384,256]{2,1,0:T(8,128)(2,1)} %collective-permute-done.6.refs_3_.refs_5_), channel_id=1, source_target_pairs={{0,1},{1,0},{2,3},{3,2},{4,5},{5,4},{6,7},{7,6},{8,9},{9,8},{10,11... | collective-permute-start | bytes 2359304 | tf_op jit(solution)/shard_map/ppermute | solution.py:269
  47.4 10.4 %copy-start.1 = (bf16[8,384,256]{2,1,0:T(8,128)(2,1)}, bf16[8,384,256]{2,1,0:T(8,128)(2,1)S(1)}, u32[]{:S(2)}) copy-start(bf16[8,384,256]{2,1,0:T(8,128)(2,1)S(1)} %collective-permute-done.11.refs_1_.refs_3_) | copy-start | bytes 4718596
  47.4 9.6 %collective-permute-start.12 = (bf16[8,384,256]{2,1,0:T(8,128)(2,1)S(1)}, bf16[8,384,256]{2,1,0:T(8,128)(2,1)S(1)}, u32[]{:S(2)}, u32[]{:S(2)}) collective-permute-start(bf16[8,384,256]{2,1,0:T(8,128)(2,1)S(1)} %collective-permute-done.11.refs_1_.refs_3_), channel_id=1, source_target_pairs={{0,1},{1,0},{2,3},{3,2},{4,5},{5,4},{6,7},{7,6},{8,9},{9,8},{10,11... | collective-permute-start | bytes 4718600 | tf_op jit(solution)/shard_map/ppermute | solution.py:269
  49.8 6.4 %collective-permute-start.15 = (bf16[4,384,256]{2,1,0:T(8,128)(2,1)}, bf16[4,384,256]{2,1,0:T(8,128)(2,1)S(1)}, u32[]{:S(2)}, u32[]{:S(2)}) collective-permute-start(bf16[4,384,256]{2,1,0:T(8,128)(2,1)} %collective-permute-done.5.refs_7_.refs_9_), channel_id=1, source_target_pairs={{0,1},{1,0},{2,3},{3,2},{4,5},{5,4},{6,7},{7,6},{8,9},{9,8},{10,11... | collective-permute-start | bytes 2359304 | tf_op jit(solution)/shard_map/ppermute | solution.py:269
  50.5 6.4 %collective-permute-start.14 = (bf16[4,384,256]{2,1,0:T(8,128)(2,1)}, bf16[4,384,256]{2,1,0:T(8,128)(2,1)S(1)}, u32[]{:S(2)}, u32[]{:S(2)}) collective-permute-start(bf16[4,384,256]{2,1,0:T(8,128)(2,1)} %collective-permute-done.8.refs_4_.refs_6_), channel_id=1, source_target_pairs={{0,1},{1,0},{2,3},{3,2},{4,5},{5,4},{6,7},{7,6},{8,9},{9,8},{10,11... | collective-permute-start | bytes 2359304 | tf_op jit(solution)/shard_map/ppermute | solution.py:269
  50.5 7.3 %copy-start.3 = (bf16[4,384,256]{2,1,0:T(8,128)(2,1)}, bf16[4,384,256]{2,1,0:T(8,128)(2,1)S(1)}, u32[]{:S(2)}) copy-start(bf16[4,384,256]{2,1,0:T(8,128)(2,1)S(1)} %collective-permute-done.13.refs_5_.refs_7_) | copy-start | bytes 2359300
  50.5 6.5 %collective-permute-start.16 = (bf16[4,384,256]{2,1,0:T(8,128)(2,1)}, bf16[4,384,256]{2,1,0:T(8,128)(2,1)S(1)}, u32[]{:S(2)}, u32[]{:S(2)}) collective-permute-start(bf16[4,384,256]{2,1,0:T(8,128)(2,1)} %collective-permute-done.7.refs_8_.refs_10_), channel_id=1, source_target_pairs={{0,1},{1,0},{2,3},{3,2},{4,5},{5,4},{6,7},{7,6},{8,9},{9,8},{10,11... | collective-permute-start | bytes 2359304 | tf_op jit(solution)/shard_map/ppermute | solution.py:269
  56.3 1.5 copy-start.4
  56.3 74.2 %collective-permute-start.18 = (bf16[4,384,256]{2,1,0:T(8,128)(2,1)}, bf16[4,384,256]{2,1,0:T(8,128)(2,1)S(1)}, u32[]{:S(2)}, u32[]{:S(2)}) collective-permute-start(bf16[4,384,256]{2,1,0:T(8,128)(2,1)} %get-tuple-element.29), channel_id=1, source_target_pairs={{14,8},{15,9},{12,10},{13,11},{30,24},{31,25},{28,26},{29,27}} | collective-permute-start | bytes 2359304 | tf_op jit(solution)/shard_map/ppermute | solution.py:269
  57.0 1.7 copy-start.2
  58.7 15.1 %copy-start.12 = (bf16[4,384,256]{2,1,0:T(8,128)(2,1)S(1)}, bf16[4,384,256]{2,1,0:T(8,128)(2,1)}, u32[]{:S(2)}) copy-start(bf16[4,384,256]{2,1,0:T(8,128)(2,1)} %get-tuple-element.26) | copy-start | bytes 2359300
  73.7 56.7 %collective-permute-start.17 = (bf16[4,384,256]{2,1,0:T(8,128)(2,1)}, bf16[4,384,256]{2,1,0:T(8,128)(2,1)S(1)}, u32[]{:S(2)}, u32[]{:S(2)}) collective-permute-start(bf16[4,384,256]{2,1,0:T(8,128)(2,1)} %collective-permute-done.10.refs_0_.refs_15_), channel_id=1, source_target_pairs={{0,1},{1,0},{2,3},{3,2},{4,5},{5,4},{6,7},{7,6},{8,9},{9,8},{10,11... | collective-permute-start | bytes 2359304 | tf_op jit(solution)/shard_map/ppermute | solution.py:313
  73.8 71.9 %collective-permute-start.9 = (bf16[4,384,256]{2,1,0:T(8,128)(2,1)S(1)}, bf16[4,384,256]{2,1,0:T(8,128)(2,1)S(1)}, u32[]{:S(2)}, u32[]{:S(2)}) collective-permute-start(bf16[4,384,256]{2,1,0:T(8,128)(2,1)S(1)} %copy-done.12), channel_id=1, source_target_pairs={{0,8},{1,9},{2,10},{3,11},{16,24},{17,25},{18,26},{19,27}} | collective-permute-start | bytes 2359304 | tf_op jit(solution)/shard_map/ppermute | solution.py:269
  129.7 17.2 %collective-permute-start.20 = (bf16[4,384,256]{2,1,0:T(8,128)(2,1)S(1)}, bf16[4,384,256]{2,1,0:T(8,128)(2,1)S(1)}, u32[]{:S(2)}, u32[]{:S(2)}) collective-permute-start(bf16[4,384,256]{2,1,0:T(8,128)(2,1)S(1)} %copy-done.12), channel_id=1, source_target_pairs={{14,8},{15,9},{12,10},{13,11},{30,24},{31,25},{28,26},{29,27}} | collective-permute-start | bytes 2359304 | tf_op jit(solution)/shard_map/ppermute | solution.py:269
  145.7 2.3 %copy-start.9 = (bf16[4,384,256]{2,1,0:T(8,128)(2,1)}, bf16[4,384,256]{2,1,0:T(8,128)(2,1)S(1)}, u32[]{:S(2)}) copy-start(bf16[4,384,256]{2,1,0:T(8,128)(2,1)S(1)} %collective-permute-done.9.refs_0_) | copy-start | bytes 2359300
  145.7 2.3 %collective-permute-start.19 = (bf16[4,384,256]{2,1,0:T(8,128)(2,1)S(1)}, bf16[4,384,256]{2,1,0:T(8,128)(2,1)S(1)}, u32[]{:S(2)}, u32[]{:S(2)}) collective-permute-start(bf16[4,384,256]{2,1,0:T(8,128)(2,1)S(1)} %collective-permute-done.9.refs_0_), channel_id=1, source_target_pairs={{0,1},{1,0},{2,3},{3,2},{4,5},{5,4},{6,7},{7,6},{8,9},{9,8},{10,11... | collective-permute-start | bytes 2359304 | tf_op jit(solution)/shard_map/ppermute | solution.py:313
  (6 other events, 6.1 us)
